TPU v7x, 256 devices: a whole 4x4x8 slice. The times are simulated.
256 devices in a mesh: ctx: 32 (over z, x), head: 8 (over y, core).
Axes of the slice: x: 4, y: 4, z: 8, core: 2. Of those that a mesh axis runs over, the one named last changes fastest.
Arguments:
- queries: bfloat16 [4096, 4096], P(('ctx', 'head')), may hold values from -48 to 48
- keys: bfloat16 [32768, 1024], P('ctx', 'head'), may hold values from -4.5 to 4.5
- values: bfloat16 [32768, 1024], P('ctx', 'head'), may hold values from -5 to 5
- grad_out: bfloat16 [4096, 4096], P(('ctx', 'head')), may hold values from -5 to 5
- gates: int32 [4096, 8, 3], P('ctx', 'head'), may hold values from 0 to 31, as said below
- block_order: int32 [32], replicated, may hold values from 0 to 31, as said below
Outputs:
- attn_out: bfloat16 [4096, 4096], P(('ctx', 'head'))
- grad_queries: bfloat16 [4096, 4096], P(('ctx', 'head'))
- grad_keys: bfloat16 [32768, 1024], P('ctx', 'head')
- grad_values: bfloat16 [32768, 1024], P('ctx', 'head')
Inputs may be any that keep to these rules, and one draw needn't show every extreme that they name: A permutation: slot s holds block block_order[s]. gates[r, h, 0] is the block of query row r. Entries 1 and 2 are blocks before it and differ from each other, or equal entry 0 to mean no block. Over the rows of one device and one key head, at most 16 of entries 1 and 2 name any one block, and at most 8 name any block other than the block that entries 1 and 2 name most often over all rows and key heads; both bounds are reached.
All inputs are finite; a program needn't handle non-finite values.
Results may differ from a plain program's by a relative error of at most 0.025.
Values may be sent and summed in bfloat16 or wider, within the bound.
No kernel may reach another device: no remote copies, remote signals or barrier semaphores. Data moves between devices by JAX's collectives and lax.ppermute only.
A program may use at most 64 MiB of HBM per device.

v0:
```python
import jax
import jax.numpy as jnp
from jax import lax
from jax.sharding import PartitionSpec as P

DH = 128
HQ = 32
KVH = 8
BS = 1024
QB = 128
BLK_DEV = 1
CAP = 16


NEG_FILL = -1e30


def block_partial(query_row_list, key_block_tile, value_block_tile, allowed):
    softmax_scale = DH ** (-0.5)
    scores = (
        jnp.einsum(
            "fsql,csl->fsqc", query_row_list, key_block_tile, preferred_element_type=jnp.float32
        )
        * softmax_scale
    )
    if allowed is not None:
        scores = jnp.where(allowed, scores, NEG_FILL)
    top_score = jnp.max(scores, axis=-1, keepdims=True)
    weights = jnp.exp(scores - top_score)
    total_weight = jnp.sum(weights, axis=-1, keepdims=True)
    probability_half = (weights / total_weight).astype(jnp.bfloat16)
    partial_value = jnp.einsum(
        "twxp,pwh->twxh", probability_half, value_block_tile, preferred_element_type=jnp.float32
    )
    return (partial_value, (top_score + jnp.log(total_weight))[..., 0])


def block_grads(
    query_row_list, gradient_row_list, logsum, delta_row, key_block_tile, value_block_tile, allowed
):
    softmax_scale = DH ** (-0.5)
    scores = (
        jnp.einsum(
            "fsql,csl->fsqc", query_row_list, key_block_tile, preferred_element_type=jnp.float32
        )
        * softmax_scale
    )
    if allowed is not None:
        scores = jnp.where(allowed, scores, NEG_FILL)
    gate_matrix = jnp.exp(scores - logsum[..., None])
    grad_v = jnp.einsum(
        "zhsc,zhsr->chr",
        gate_matrix.astype(jnp.bfloat16),
        gradient_row_list,
        preferred_element_type=jnp.float32,
    )
    probability_gradient = jnp.einsum(
        "fsql,csl->fsqc", gradient_row_list, value_block_tile, preferred_element_type=jnp.float32
    )
    score_gradient = (gate_matrix * (probability_gradient - delta_row[..., None])).astype(
        jnp.bfloat16
    )
    grad_k = (
        jnp.einsum(
            "zhsc,zhsr->chr", score_gradient, query_row_list, preferred_element_type=jnp.float32
        )
        * softmax_scale
    )
    grad_q = (
        jnp.einsum(
            "twxp,pwh->twxh", score_gradient, key_block_tile, preferred_element_type=jnp.float32
        )
        * softmax_scale
    ).astype(jnp.bfloat16)
    return (grad_q, grad_k, grad_v)


def per_block(tensor, blk_index, capacity):
    split_view = tensor.reshape((tensor.shape[0], BLK_DEV, capacity) + tensor.shape[2:])
    return split_view[:, blk_index].reshape((tensor.shape[0] * capacity,) + tensor.shape[2:])


def join_blocks(pieces, ctx_count, capacity):
    shaped = [piece.reshape((ctx_count, capacity) + piece.shape[1:]) for piece in pieces]
    stacked = jnp.stack(shaped, axis=1)
    return stacked.reshape((ctx_count, BLK_DEV * capacity) + stacked.shape[3:])


def on_device(queries, keys, values, grad_out, gates, block_order):
    ctx_index = lax.axis_index("ctx")
    ctx_count = lax.axis_size("ctx")
    q_rows, do_rows = (
        lax.all_to_all(queries, "head", split_axis=1, concat_axis=0, tiled=True),
        lax.all_to_all(grad_out, "head", split_axis=1, concat_axis=0, tiled=True),
    )
    row_count = q_rows.shape[0]
    kv_dev = keys.shape[1] // DH
    group_size = HQ // KVH
    row_width = group_size * DH
    block_total = block_order.shape[0]
    query4 = q_rows.reshape(row_count, kv_dev, group_size, DH)
    grad4 = do_rows.reshape(row_count, kv_dev, group_size, DH)
    key_blocks = keys.reshape(BLK_DEV, BS, kv_dev, DH)
    val_blocks = values.reshape(BLK_DEV, BS, kv_dev, DH)
    block_ids = jnp.arange(block_total, dtype=jnp.int32)
    slot_match = block_order[:, None] == block_ids[None, :]
    slot_of = jnp.sum(jnp.where(slot_match, block_ids[:, None], 0), axis=0)
    local_order = lax.dynamic_slice_in_dim(block_order, ctx_index * BLK_DEV, BLK_DEV)
    own_block = jnp.repeat(local_order, QB)
    remote = gates[:, :, 1:]
    present = remote != own_block[:, None, None]
    remote_match = remote[..., None] == block_ids
    target = jnp.sum(jnp.where(remote_match, slot_of, 0), axis=-1)
    capacity = CAP
    flat_target = target.transpose(1, 0, 2).reshape(kv_dev, row_count * 2)
    flat_routed = present.transpose(1, 0, 2).reshape(kv_dev, row_count * 2)
    onehot = jnp.where(
        flat_routed[..., None], (flat_target[..., None] == block_ids).astype(jnp.int32), 0
    )
    slot_rank = jnp.sum((jnp.cumsum(onehot, axis=1) - 1) * onehot, axis=-1)
    dump_slot = block_total * capacity
    position = jnp.where(flat_routed, flat_target * capacity + slot_rank, dump_slot)
    heads_index = jnp.broadcast_to(jnp.arange(kv_dev)[:, None], position.shape)
    row_index = (jnp.arange(row_count * 2) // 2)[None, :]
    source_row = (
        jnp.full((kv_dev, dump_slot + 1), row_count, jnp.int32)
        .at[heads_index, position]
        .set(row_index)[:, :dump_slot]
    )
    slot_heads = jnp.arange(kv_dev)[None, :]

    def pack(tensor):
        padded = jnp.concatenate([tensor, jnp.zeros((1,) + tensor.shape[1:], tensor.dtype)], axis=0)
        picked = padded[source_row.T, slot_heads]
        return picked.reshape((ctx_count, BLK_DEV * capacity) + tensor.shape[1:])

    def unpack(tensor, fill_value):
        flat_rows = tensor.reshape((dump_slot,) + tensor.shape[2:])
        padded = jnp.concatenate(
            [flat_rows, jnp.full((1,) + flat_rows.shape[1:], fill_value, flat_rows.dtype)], axis=0
        )
        picked = padded[position, heads_index].reshape((kv_dev, row_count, 2) + flat_rows.shape[2:])
        return jnp.moveaxis(picked, 0, 2)

    got_q = lax.all_to_all(
        pack(q_rows.reshape(row_count, kv_dev, row_width)),
        "ctx",
        split_axis=0,
        concat_axis=0,
        tiled=True,
    )
    causal = (jnp.arange(BS)[None, :] <= (BS - QB + jnp.arange(QB))[:, None])[:, None, None, :]
    own_parts = [block_partial(query4, key_blocks[0], val_blocks[0], causal)]
    own_out = jnp.concatenate([piece[0] for piece in own_parts], axis=0)
    own_lse = jnp.concatenate([piece[1] for piece in own_parts], axis=0)
    item_q = per_block(got_q, 0, capacity).reshape(ctx_count * capacity, kv_dev, group_size, DH)
    far_parts = [block_partial(item_q, key_blocks[0], val_blocks[0], None)]
    far_out = join_blocks(
        [piece[0].reshape(ctx_count * capacity, kv_dev, row_width) for piece in far_parts],
        ctx_count,
        capacity,
    )
    far_lse = join_blocks([piece[1] for piece in far_parts], ctx_count, capacity)
    back_out, back_lse = (
        lax.all_to_all(
            far_out.astype(jnp.bfloat16), "ctx", split_axis=0, concat_axis=0, tiled=True
        ).astype(far_out.dtype),
        lax.all_to_all(
            far_lse.astype(jnp.bfloat16), "ctx", split_axis=0, concat_axis=0, tiled=True
        ).astype(far_lse.dtype),
    )
    remote_out = unpack(back_out, 0.0).reshape(row_count, 2, kv_dev, group_size, DH)
    remote_lse = unpack(back_lse, NEG_FILL)
    all_lse = jnp.concatenate([own_lse[:, None], remote_lse], axis=1)
    all_out = jnp.concatenate([own_out[:, None], remote_out], axis=1)
    top_lse = jnp.max(all_lse, axis=1, keepdims=True)
    logsum = top_lse + jnp.log(jnp.sum(jnp.exp(all_lse - top_lse), axis=1, keepdims=True))
    attention = jnp.sum(jnp.exp(all_lse - logsum)[..., None] * all_out, axis=1).astype(jnp.bfloat16)
    logsum = logsum[:, 0]
    delta_row = jnp.sum(grad4.astype(jnp.float32) * attention.astype(jnp.float32), axis=-1)
    got_do = lax.all_to_all(
        pack(do_rows.reshape(row_count, kv_dev, row_width)),
        "ctx",
        split_axis=0,
        concat_axis=0,
        tiled=True,
    )
    got_lse, got_delta = (
        lax.all_to_all(pack(logsum), "ctx", split_axis=0, concat_axis=0, tiled=True),
        lax.all_to_all(pack(delta_row), "ctx", split_axis=0, concat_axis=0, tiled=True),
    )
    dq_own, dk_own, dv_own = block_grads(
        query4, grad4, logsum, delta_row, key_blocks[0], val_blocks[0], causal
    )
    item_do = per_block(got_do, 0, capacity).reshape(ctx_count * capacity, kv_dev, group_size, DH)
    item_lse = per_block(got_lse, 0, capacity)
    item_delta = per_block(got_delta, 0, capacity)
    dq_far, dk_far, dv_far = block_grads(
        item_q, item_do, item_lse, item_delta, key_blocks[0], val_blocks[0], None
    )
    key_grads = [dk_own + dk_far]
    val_grads = [dv_own + dv_far]
    far_dq = [dq_far.reshape(ctx_count * capacity, kv_dev, row_width)]
    back_dq = lax.all_to_all(
        join_blocks(far_dq, ctx_count, capacity), "ctx", split_axis=0, concat_axis=0, tiled=True
    )
    remote_dq = unpack(back_dq, 0.0).reshape(row_count, 2, kv_dev, group_size, DH)
    key_grad_all = jnp.stack(key_grads, axis=0)
    val_grad_all = jnp.stack(val_grads, axis=0)
    dq_total = dq_own.astype(jnp.float32) + jnp.sum(remote_dq.astype(jnp.float32), axis=1)
    grad_queries_rows = dq_total.astype(jnp.bfloat16).reshape(row_count, kv_dev * row_width)
    attn_tokens, dq_tokens = (
        lax.all_to_all(
            attention.reshape(row_count, kv_dev * row_width),
            "head",
            split_axis=0,
            concat_axis=1,
            tiled=True,
        ),
        lax.all_to_all(grad_queries_rows, "head", split_axis=0, concat_axis=1, tiled=True),
    )
    grad_keys = key_grad_all.astype(jnp.bfloat16).reshape(BLK_DEV * BS, kv_dev * DH)
    grad_values = val_grad_all.astype(jnp.bfloat16).reshape(BLK_DEV * BS, kv_dev * DH)
    return (attn_tokens, dq_tokens, grad_keys, grad_values)


def solution(mesh):
    return jax.shard_map(
        on_device,
        mesh=mesh,
        in_specs=(
            P(("ctx", "head"), None),
            P("ctx", "head"),
            P("ctx", "head"),
            P(("ctx", "head"), None),
            P("ctx", "head", None),
            P(),
        ),
        out_specs=(
            P(("ctx", "head"), None),
            P(("ctx", "head"), None),
            P("ctx", "head"),
            P("ctx", "head"),
        ),
        check_vma=False,
    )
```

profile of v0, /device:TPU:1, one launch (start us, length us, event | category | flops | bytes accessed | tf_op | source)
XLA Modules:
  0.0 209.9 jit_solution(4069008953780379438)
XLA Ops:
  2.3 6.5 %all-to-all-start = ((bf16[16,8,512]{2,0,1:T(8,128)(2,1)}), bf16[16,8,512]{2,0,1:T(8,128)(2,1)S(1)}, u32[]{:S(2)}, u32[]{:S(2)}) async-start(bf16[16,8,512]{2,0,1:T(8,128)(2,1)} %bitcast.322), calls=%async_computation | async-start | bytes 262144 | tf_op jit(solution)/shard_map/all_to_all | solution.py:93
  18.2 4.8 %all-to-all-start.5 = ((bf16[16,8,512]{2,0,1:T(8,128)(2,1)}), bf16[16,8,512]{2,0,1:T(8,128)(2,1)S(1)}, u32[]{:S(2)}, u32[]{:S(2)}) async-start(bf16[16,8,512]{2,0,1:T(8,128)(2,1)} %bitcast.321), calls=%async_computation.5 | async-start | bytes 262144 | tf_op jit(solution)/shard_map/all_to_all | solution.py:94
  23.0 5.8 %gather_fusion = bf16[512,512]{1,0:T(8,128)(2,1)} fusion(bf16[129,1,512]{2,0,1:T(8,128)(2,1)S(1)} %concatenate.75, s32[512]{0:T(512)S(1)} %bitcast.324), kind=kCustom, calls=%fused_computation | custom fusion | bytes 1052672 | tf_op jit(solution)/shard_map/gather | solution.py:134
  28.9 10.5 %all-to-all-start.1 = ((bf16[32,16,1,512]{3,1,2,0:T(8,128)(2,1)}), bf16[32,16,1,512]{3,1,2,0:T(8,128)(2,1)S(1)}, u32[]{:S(2)}, u32[]{:S(2)}) async-start(bf16[32,16,1,512]{3,1,2,0:T(8,128)(2,1)} %bitcast.22), calls=%async_computation.1 | async-start | bytes 1048576 | tf_op jit(solution)/shard_map/all_to_all | solution.py:145
  39.4 5.8 %gather_fusion.4 = bf16[512,512]{1,0:T(8,128)(2,1)} fusion(bf16[129,1,512]{2,0,1:T(8,128)(2,1)S(1)} %concatenate.90, s32[512]{0:T(512)S(1)} %bitcast.325), kind=kCustom, calls=%fused_computation.4 | custom fusion | bytes 1052672 | tf_op jit(solution)/shard_map/gather | solution.py:134
  48.1 7.8 %all-to-all-done.1 = bf16[32,16,1,512]{3,1,2,0:T(8,128)(2,1)S(1)} async-done(((bf16[32,16,1,512]{3,1,2,0:T(8,128)(2,1)}), bf16[32,16,1,512]{3,1,2,0:T(8,128)(2,1)S(1)}, u32[]{:S(2)}, u32[]{:S(2)}) %all-to-all-start.1) | async-done | bytes 524320 | tf_op jit(solution)/shard_map/all_to_all | solution.py:145
  55.9 5.0 %all-to-all-start.7 = ((bf16[32,16,1,512]{3,1,2,0:T(8,128)(2,1)}), bf16[32,16,1,512]{3,1,2,0:T(8,128)(2,1)S(1)}, u32[]{:S(2)}, u32[]{:S(2)}) async-start(bf16[32,16,1,512]{3,1,2,0:T(8,128)(2,1)} %bitcast.60), calls=%async_computation.7 | async-start | bytes 1048576 | tf_op jit(solution)/shard_map/all_to_all | solution.py:181
  64.5 1.9 fusion.6
  68.4 7.5 %all-to-all-done.7 = bf16[32,16,1,512]{3,1,2,0:T(8,128)(2,1)S(1)} async-done(((bf16[32,16,1,512]{3,1,2,0:T(8,128)(2,1)}), bf16[32,16,1,512]{3,1,2,0:T(8,128)(2,1)S(1)}, u32[]{:S(2)}, u32[]{:S(2)}) %all-to-all-start.7) | async-done | bytes 524320 | tf_op jit(solution)/shard_map/all_to_all | solution.py:181
  76.0 6.5 %all-to-all-start.2 = ((bf16[32,16,1,4]{1,3,2,0:T(4,128)(2,1)}), bf16[32,16,1,4]{1,3,2,0:T(4,128)(2,1)}, u32[]{:S(2)}, u32[]{:S(2)}) async-start(bf16[32,16,1,4]{1,3,2,0:T(4,128)(2,1)} %copy.356), calls=%async_computation.2 | async-start | bytes 65536 | tf_op jit(solution)/shard_map/all_to_all | solution.py:168
  82.5 5.2 %fusion.30 = bf16[512,1,4,128]{3,0,2,1:T(8,128)(2,1)S(1)} fusion(f32[512,4]{0,1:T(4,128)S(1)} %fusion.6, f32[512,4]{0,1:T(4,128)S(1)} %get-tuple-element.8, f32[512,4,1024]{2,0,1:T(8,128)} %copy-done.1, bf16[1024,128]{1,0:T(8,128)(2,1)S(1)} %copy-done.10), kind=kOutput, calls=%fused_computation.48 | convolution fusion | flops 545521664 | bytes 9191424 | tf_op jit(solution)/shard_map/twxp,pwh->twxh/dot_general | solution.py:32
  89.2 1.8 all-to-all-done.2
  91.0 7.6 %all-to-all-start.3 = ((bf16[32,16,1,512]{3,1,2,0:T(8,128)(2,1)}), bf16[32,16,1,512]{3,1,2,0:T(8,128)(2,1)S(1)}, u32[]{:S(2)}, u32[]{:S(2)}) async-start(bf16[32,16,1,512]{3,1,2,0:T(8,128)(2,1)} %bitcast.44), calls=%async_computation.3 | async-start | bytes 1048576 | tf_op jit(solution)/shard_map/all_to_all | solution.py:165
  100.0 1.7 reshape.833
  101.7 1.8 copy.368
  104.4 2.2 %copy.391 = bf16[512,4,128]{0,2,1:T(8,128)(2,1)} copy(bf16[512,4,128]{2,1,0:T(4,128)(2,1)} %reshape.825) | data formatting | bytes 1048576 | tf_op jit(solution)/shard_map/reshape.64
  109.3 1.6 gather_fusion.3
  113.0 9.0 %all-to-all-start.6 = ((f32[32,16,1,4]{1,3,2,0:T(4,128)}), f32[32,16,1,4]{1,3,2,0:T(4,128)}, u32[]{:S(2)}, u32[]{:S(2)}) async-start(f32[32,16,1,4]{1,3,2,0:T(4,128)} %copy.376), calls=%async_computation.6 | async-start | bytes 131072 | tf_op jit(solution)/shard_map/all_to_all | solution.py:189
  124.0 2.0 gather_fusion.2
  127.2 1.7 fusion.53
  133.3 9.3 %all-to-all-start.8 = ((f32[32,16,1,4]{1,3,2,0:T(4,128)}), f32[32,16,1,4]{1,3,2,0:T(4,128)}, u32[]{:S(2)}, u32[]{:S(2)}) async-start(f32[32,16,1,4]{1,3,2,0:T(4,128)} %copy.380), calls=%async_computation.8 | async-start | bytes 131072 | tf_op jit(solution)/shard_map/all_to_all | solution.py:190
  146.1 5.3 %all-to-all-done.8 = f32[32,16,1,4]{1,3,2,0:T(4,128)} async-done(((f32[32,16,1,4]{1,3,2,0:T(4,128)}), f32[32,16,1,4]{1,3,2,0:T(4,128)}, u32[]{:S(2)}, u32[]{:S(2)}) %all-to-all-start.8) | async-done | bytes 8224 | tf_op jit(solution)/shard_map/all_to_all | solution.py:190
  154.4 4.9 %fusion.8 = bf16[512,4,1024]{2,0,1:T(8,128)(2,1)S(1)} fusion(f32[512,4,1024]{2,0,1:T(8,128)} %copy-done.1, f32[512,4]{0,1:T(4,128)} %sub.119, f32[512,4]{0,1:T(4,128)} %sub.116, bf16[512,4,128]{0,2,1:T(8,128)(2,1)S(1)} %copy-done.3, bf16[1024,128]{1,0:T(8,128)(2,1)} %param.8), kind=kOutput, calls=%fused_computation.21 | convolution fusion | flops 547356672 | bytes 13385728 | tf_op jit(solution)/shard_map/fsql,csl->fsqc/dot_general | solution.py:57
  159.3 2.0 copy-done.2
  163.8 2.1 reshape_stack_reshape_reshape.4
  165.9 4.8 %all-to-all-start.9 = ((bf16[32,16,1,512]{3,1,2,0:T(8,128)(2,1)}), bf16[32,16,1,512]{3,1,2,0:T(8,128)(2,1)}, u32[]{:S(2)}, u32[]{:S(2)}) async-start(bf16[32,16,1,512]{3,1,2,0:T(8,128)(2,1)} %bitcast.337), calls=%async_computation.9 | async-start | bytes 1048576 | tf_op jit(solution)/shard_map/all_to_all | solution.py:204
  170.7 6.3 %fusion.41 = bf16[1024,128]{1,0:T(8,128)(2,1)} fusion(f32[128,1024]{0,1:T(8,128)S(1)} %convolution_bitcast_fusion, bf16[512,4,128]{0,2,1:T(8,128)(2,1)S(1)} %copy-done.3, f32[512,4,1024]{2,0,1:T(8,128)} %copy-done.1, f32[512,4]{0,1:T(4,128)} %sub.116), kind=kOutput, calls=%fused_computation.54 | convolution fusion | flops 543424512 | bytes 9707520 | tf_op jit(solution)/shard_map/zhsc,zhsr->chr/dot_general | solution.py:51
  181.0 4.1 %fusion.29 = f32[128,1024]{0,1:T(8,128)S(1)} fusion(bf16[512,4,128]{0,2,1:T(8,128)(2,1)} %copy-done.4, bf16[512,4,1024]{2,0,1:T(8,128)(2,1)} %copy-done.2), kind=kOutput, calls=%fused_computation.47 | convolution fusion | flops 537001984 | bytes 5242880 | tf_op jit(solution)/shard_map/zhsc,zhsr->chr/dot_general | solution.py:64
  185.2 9.4 %all-to-all-start.4 = ((bf16[8,16,512]{2,1,0:T(8,128)(2,1)}), bf16[8,16,512]{2,1,0:T(8,128)(2,1)S(1)}, u32[]{:S(2)}, u32[]{:S(2)}) async-start(bf16[8,16,512]{2,1,0:T(8,128)(2,1)} %convert_element_type.205), calls=%async_computation.4 | async-start | bytes 262144 | tf_op jit(solution)/shard_map/all_to_all | solution.py:213
  195.6 1.8 gather_fusion.6
  199.8 4.2 %all-to-all-start.10 = ((bf16[8,16,512]{2,1,0:T(8,128)(2,1)}), bf16[8,16,512]{2,1,0:T(8,128)(2,1)S(1)}, u32[]{:S(2)}, u32[]{:S(2)}) async-start(bf16[8,16,512]{2,1,0:T(8,128)(2,1)} %all_to_all.87), calls=%async_computation.10 | async-start | bytes 262144 | tf_op jit(solution)/shard_map/all_to_all | solution.py:220
  205.8 3.5 %all-to-all-done.10 = bf16[8,16,512]{2,1,0:T(8,128)(2,1)S(1)} async-done(((bf16[8,16,512]{2,1,0:T(8,128)(2,1)}), bf16[8,16,512]{2,1,0:T(8,128)(2,1)S(1)}, u32[]{:S(2)}, u32[]{:S(2)}) %all-to-all-start.10) | async-done | bytes 131104 | tf_op jit(solution)/shard_map/all_to_all | solution.py:220
  (134 shorter events, 54.5 us)
Async XLA Ops:
  0.6 44.6 %copy-start = (bf16[1024,128]{1,0:T(8,128)(2,1)S(1)}, bf16[1024,128]{1,0:T(8,128)(2,1)}, u32[]{:S(2)}) copy-start(bf16[1024,128]{1,0:T(8,128)(2,1)} %param.7) | copy-start | bytes 786436
  2.3 15.9 %all-to-all-start = ((bf16[16,8,512]{2,0,1:T(8,128)(2,1)}), bf16[16,8,512]{2,0,1:T(8,128)(2,1)S(1)}, u32[]{:S(2)}, u32[]{:S(2)}) async-start(bf16[16,8,512]{2,0,1:T(8,128)(2,1)} %bitcast.322), calls=%async_computation | async-start | bytes 262144 | tf_op jit(solution)/shard_map/all_to_all | solution.py:93
  18.2 10.7 %all-to-all-start.5 = ((bf16[16,8,512]{2,0,1:T(8,128)(2,1)}), bf16[16,8,512]{2,0,1:T(8,128)(2,1)S(1)}, u32[]{:S(2)}, u32[]{:S(2)}) async-start(bf16[16,8,512]{2,0,1:T(8,128)(2,1)} %bitcast.321), calls=%async_computation.5 | async-start | bytes 262144 | tf_op jit(solution)/shard_map/all_to_all | solution.py:94
  28.9 27.0 %all-to-all-start.1 = ((bf16[32,16,1,512]{3,1,2,0:T(8,128)(2,1)}), bf16[32,16,1,512]{3,1,2,0:T(8,128)(2,1)S(1)}, u32[]{:S(2)}, u32[]{:S(2)}) async-start(bf16[32,16,1,512]{3,1,2,0:T(8,128)(2,1)} %bitcast.22), calls=%async_computation.1 | async-start | bytes 1048576 | tf_op jit(solution)/shard_map/all_to_all | solution.py:145
  39.4 6.6 %copy-start.7 = (bf16[128,4,128]{2,1,0:T(4,128)(2,1)}, bf16[128,4,128]{2,1,0:T(4,128)(2,1)S(1)}, u32[]{:S(2)}) copy-start(bf16[128,4,128]{2,1,0:T(4,128)(2,1)S(1)} %reshape.806) | copy-start | bytes 393220
  39.4 7.4 %copy-start.9 = (bf16[1024,128]{1,0:T(8,128)(2,1)S(1)}, bf16[1024,128]{1,0:T(8,128)(2,1)}, u32[]{:S(2)}) copy-start(bf16[1024,128]{1,0:T(8,128)(2,1)} %param.8) | copy-start | bytes 786436
  45.7 0.6 copy-start.12
  46.3 0.6 copy-start.14
  55.9 20.1 %all-to-all-start.7 = ((bf16[32,16,1,512]{3,1,2,0:T(8,128)(2,1)}), bf16[32,16,1,512]{3,1,2,0:T(8,128)(2,1)S(1)}, u32[]{:S(2)}, u32[]{:S(2)}) async-start(bf16[32,16,1,512]{3,1,2,0:T(8,128)(2,1)} %bitcast.60), calls=%async_computation.7 | async-start | bytes 1048576 | tf_op jit(solution)/shard_map/all_to_all | solution.py:181
  63.1 1.4 copy-start.4
  64.5 3.2 %copy-start.1 = (f32[512,4,1024]{2,0,1:T(8,128)}, f32[512,4,1024]{2,0,1:T(8,128)S(1)}, u32[]{:S(2)}) copy-start(f32[512,4,1024]{2,0,1:T(8,128)S(1)} %get-tuple-element.9) | copy-start | bytes 25165828
  64.5 18.0 %copy-start.10 = (bf16[1024,128]{1,0:T(8,128)(2,1)S(1)}, bf16[1024,128]{1,0:T(8,128)(2,1)}, u32[]{:S(2)}) copy-start(bf16[1024,128]{1,0:T(8,128)(2,1)} %param.8) | copy-start | bytes 786436
  76.0 15.0 %all-to-all-start.2 = ((bf16[32,16,1,4]{1,3,2,0:T(4,128)(2,1)}), bf16[32,16,1,4]{1,3,2,0:T(4,128)(2,1)}, u32[]{:S(2)}, u32[]{:S(2)}) async-start(bf16[32,16,1,4]{1,3,2,0:T(4,128)(2,1)} %copy.356), calls=%async_computation.2 | async-start | bytes 65536 | tf_op jit(solution)/shard_map/all_to_all | solution.py:168
  88.1 21.0 %copy-start.13 = (f32[128,4]{0,1:T(4,128)S(1)}, f32[128,4]{0,1:T(4,128)}, u32[]{:S(2)}) copy-start(f32[128,4]{0,1:T(4,128)} %copy-done.12) | copy-start | bytes 6148
  88.1 21.0 %copy-start.15 = (f32[128,4]{0,1:T(4,128)S(1)}, f32[128,4]{0,1:T(4,128)}, u32[]{:S(2)}) copy-start(f32[128,4]{0,1:T(4,128)} %copy-done.14) | copy-start | bytes 6148
  91.0 22.1 %all-to-all-start.3 = ((bf16[32,16,1,512]{3,1,2,0:T(8,128)(2,1)}), bf16[32,16,1,512]{3,1,2,0:T(8,128)(2,1)S(1)}, u32[]{:S(2)}, u32[]{:S(2)}) async-start(bf16[32,16,1,512]{3,1,2,0:T(8,128)(2,1)} %bitcast.44), calls=%async_computation.3 | async-start | bytes 1048576 | tf_op jit(solution)/shard_map/all_to_all | solution.py:165
  113.0 20.3 %all-to-all-start.6 = ((f32[32,16,1,4]{1,3,2,0:T(4,128)}), f32[32,16,1,4]{1,3,2,0:T(4,128)}, u32[]{:S(2)}, u32[]{:S(2)}) async-start(f32[32,16,1,4]{1,3,2,0:T(4,128)} %copy.376), calls=%async_computation.6 | async-start | bytes 131072 | tf_op jit(solution)/shard_map/all_to_all | solution.py:189
  124.0 18.6 %copy-start.5 = (bf16[128,4,128]{2,1,0:T(4,128)(2,1)S(1)}, bf16[128,4,128]{2,1,0:T(4,128)(2,1)}, u32[]{:S(2)}) copy-start(bf16[128,4,128]{2,1,0:T(4,128)(2,1)} %reshape.820) | copy-start | bytes 393220
  127.2 27.2 %copy-start.3 = (bf16[512,4,128]{0,2,1:T(8,128)(2,1)S(1)}, bf16[512,4,128]{0,2,1:T(8,128)(2,1)}, u32[]{:S(2)}) copy-start(bf16[512,4,128]{0,2,1:T(8,128)(2,1)} %copy.391) | copy-start | bytes 1572868
  128.9 1.2 copy-start.6
  130.1 0.6 copy-start.11
  133.3 18.1 %all-to-all-start.8 = ((f32[32,16,1,4]{1,3,2,0:T(4,128)}), f32[32,16,1,4]{1,3,2,0:T(4,128)}, u32[]{:S(2)}, u32[]{:S(2)}) async-start(f32[32,16,1,4]{1,3,2,0:T(4,128)} %copy.380), calls=%async_computation.8 | async-start | bytes 131072 | tf_op jit(solution)/shard_map/all_to_all | solution.py:190
  159.3 2.0 copy-start.2
  165.9 19.3 %all-to-all-start.9 = ((bf16[32,16,1,512]{3,1,2,0:T(8,128)(2,1)}), bf16[32,16,1,512]{3,1,2,0:T(8,128)(2,1)}, u32[]{:S(2)}, u32[]{:S(2)}) async-start(bf16[32,16,1,512]{3,1,2,0:T(8,128)(2,1)} %bitcast.337), calls=%async_computation.9 | async-start | bytes 1048576 | tf_op jit(solution)/shard_map/all_to_all | solution.py:204
  185.1 18.8 %copy-start.8 = (bf16[128,4,128]{2,1,0:T(4,128)(2,1)S(1)}, bf16[128,4,128]{2,1,0:T(4,128)(2,1)}, u32[]{:S(2)}) copy-start(bf16[128,4,128]{2,1,0:T(4,128)(2,1)} %copy-done.7) | copy-start | bytes 393220
  185.2 14.7 %all-to-all-start.4 = ((bf16[8,16,512]{2,1,0:T(8,128)(2,1)}), bf16[8,16,512]{2,1,0:T(8,128)(2,1)S(1)}, u32[]{:S(2)}, u32[]{:S(2)}) async-start(bf16[8,16,512]{2,1,0:T(8,128)(2,1)} %convert_element_type.205), calls=%async_computation.4 | async-start | bytes 262144 | tf_op jit(solution)/shard_map/all_to_all | solution.py:213
  199.8 9.4 %all-to-all-start.10 = ((bf16[8,16,512]{2,1,0:T(8,128)(2,1)}), bf16[8,16,512]{2,1,0:T(8,128)(2,1)S(1)}, u32[]{:S(2)}, u32[]{:S(2)}) async-start(bf16[8,16,512]{2,1,0:T(8,128)(2,1)} %all_to_all.87), calls=%async_computation.10 | async-start | bytes 262144 | tf_op jit(solution)/shard_map/all_to_all | solution.py:220
where the time goes:
time: 212 us; the launch traced here: 210 us
  starting transfers between devices  77.5 us (37%)
  local copies, waits for them, and re-layouts  65.5 us (31%)
  matrix products  28.4 us (13%)
  waiting for transfers between devices  26.9 us (13%)
  other arithmetic  10.4 us (5%)
    gather x4, local copies, waits for them, and re-layouts, pack(): picked = padded[source_row.T, slot_heads]  14.8 us
    all_to_all x1, starting transfers between devices, on_device(): lax.all_to_all(pack(q_rows.reshape(row_count, kv_dev, row_width)), 'ctx',...  10.5 us
    all_to_all x1, starting transfers between devices, on_device(): lax.all_to_all(attention.reshape(row_count, kv_dev * row_width), 'head',...  9.4 us
    all_to_all x1, starting transfers between devices, on_device(): lax.all_to_all(pack(delta_row), 'ctx', split_axis=0, concat_axis=0, tiled...  9.27 us
    all_to_all x1, starting transfers between devices, on_device(): lax.all_to_all(pack(logsum), 'ctx', split_axis=0, concat_axis=0, tiled=True)  9.05 us
    all_to_all x1, waiting for transfers between devices, on_device(): lax.all_to_all(pack(q_rows.reshape(row_count, kv_dev, row_width)), 'ctx',...  7.82 us
    all_to_all x1, starting transfers between devices, on_device(): lax.all_to_all(far_out.astype(jnp.bfloat16), 'ctx', split_axis=0, concat_...  7.55 us
    all_to_all x1, waiting for transfers between devices, on_device(): lax.all_to_all(pack(do_rows.reshape(row_count, kv_dev, row_width)), 'ctx'...  7.51 us
  transfers between devices with their start and end apart: 11, of which 7 were waited for; matrix products, arithmetic and copies ran while one was open for 40% of the time, Pallas kernels for 0%

commit v1 on v0

v1 whole, which is shorter than its diff:
```python
import functools

import jax
import jax.numpy as jnp
from jax import lax
from jax.experimental import pallas as pl
from jax.experimental.pallas import tpu as pltpu
from jax.sharding import PartitionSpec as P

DH = 128
HQ = 32
KVH = 8
GROUP = HQ // KVH
WIDTH = GROUP * DH
BS = 1024
QB = 128
CAP = 16
NB = 32
SLOTS = NB * CAP
SIDE = 3 * WIDTH
BACK = SIDE + 128
SCALE = DH ** (-0.5)
NEG_FILL = -1e30
BF = jnp.bfloat16
F32 = jnp.float32
VMEM_LIMIT = 56 * 1024 * 1024


def dot(a, b):
    return jnp.dot(a, b, preferred_element_type=F32)


def dot_first(a, b):
    return lax.dot_general(a, b, (((0,), (0,)), ((), ())), preferred_element_type=F32)


def split3(x):
    high = x.astype(BF)
    rest = x - high.astype(F32)
    middle = rest.astype(BF)
    low = (rest - middle.astype(F32)).astype(BF)
    return high, middle, low


def call(kernel, out_shape, **kwargs):
    return pl.pallas_call(
        kernel,
        out_shape=out_shape,
        compiler_params=pltpu.CompilerParams(vmem_limit_bytes=VMEM_LIMIT),
        **kwargs,
    )


def shape(dims, dtype):
    return jax.ShapeDtypeStruct(dims, dtype)


def pack_kernel(q_ref, do_ref, out_ref):
    for head in range(KVH):
        columns = slice(head * WIDTH, (head + 1) * WIDTH)
        out_ref[head, :, :WIDTH] = q_ref[:, columns]
        out_ref[head, :, WIDTH:] = do_ref[:, columns]


def route_kernel(gate_ref, order_ref, first_ref, second_ref):
    gates = gate_ref[...]
    order = order_ref[...]
    own = gates[:, 0:1]
    hits = []
    for entry in (1, 2):
        gate = gates[:, entry : entry + 1]
        hits.append(((gate == order) & (gate != own)).astype(F32))
    row = lax.broadcasted_iota(jnp.int32, (QB, QB), 0)
    column = lax.broadcasted_iota(jnp.int32, (QB, QB), 1)
    before = (column < row).astype(BF)
    slot = lax.broadcasted_iota(jnp.int32, (QB, NB), 1).astype(F32)
    place = lax.broadcasted_iota(jnp.int32, (QB, SLOTS), 1)
    taken = jnp.zeros((1, NB), F32)
    for hit, out_ref in zip(hits, (first_ref, second_ref)):
        rank = dot(before, hit.astype(BF)) + taken
        taken = taken + jnp.sum(hit, axis=0, keepdims=True)
        found = jnp.sum(hit, axis=1, keepdims=True)
        position = jnp.sum(hit * (slot * CAP + rank), axis=1, keepdims=True)
        position = jnp.where(found > 0.5, position, -1.0).astype(jnp.int32)
        out_ref[...] = (place == position).astype(BF)


def gather_kernel(rows_ref, first_ref, second_ref, out_ref):
    pick = first_ref[...] + second_ref[...]
    out_ref[...] = dot_first(pick, rows_ref[...]).astype(BF)


def attend(q_t, do_t, key, value, both_t, allowed):
    scores = dot(key, q_t) * SCALE
    if allowed is not None:
        scores = jnp.where(allowed, scores, NEG_FILL)
    top = jnp.max(scores, axis=0, keepdims=True)
    weights = jnp.exp(scores - top)
    total = jnp.sum(weights, axis=0, keepdims=True)
    weights = weights * (1.0 / total)
    prob = weights.astype(BF)
    sums = dot(both_t, prob)
    out_t = sums[:DH]
    key_sum_t = sums[DH:] * SCALE
    delta = jnp.sum(out_t * do_t.astype(F32), axis=0, keepdims=True)
    moved = (weights * (dot(value, do_t) - delta)).astype(BF)
    grad_t = dot(both_t[DH:], moved) * SCALE
    return prob, moved, out_t, grad_t, key_sum_t, top + jnp.log(total), delta


def own_kernel(rows_ref, key_ref, value_ref, prob_ref, moved_ref, res_ref, both_ref):
    key, value = key_ref[...], value_ref[...]
    both_ref[:DH] = value.astype(F32).T.astype(BF)
    both_ref[DH:] = key.astype(F32).T.astype(BF)
    both_t = both_ref[...]
    rows_t = rows_ref[...].astype(F32).T.astype(BF)
    q_t = jnp.concatenate([rows_t[j * DH : (j + 1) * DH] for j in range(GROUP)], axis=1)
    do_t = jnp.concatenate([rows_t[WIDTH + j * DH : WIDTH + (j + 1) * DH] for j in range(GROUP)], axis=1)
    key_at = lax.broadcasted_iota(jnp.int32, (BS, WIDTH), 0)
    row_at = lax.broadcasted_iota(jnp.int32, (BS, WIDTH), 1) % QB
    allowed = key_at <= row_at + (BS - QB)
    prob, moved, out_t, grad_t, key_sum_t, lse, delta = attend(q_t, do_t, key, value, both_t, allowed)
    prob_ref[...] = prob
    moved_ref[...] = moved
    line = lax.broadcasted_iota(jnp.int32, (DH, QB), 0)
    side_t = jnp.zeros((DH, QB), F32)
    for j in range(GROUP):
        columns = slice(j * QB, (j + 1) * QB)
        for part, piece in enumerate((out_t, grad_t, key_sum_t)):
            res_ref[:, part * WIDTH + j * DH : part * WIDTH + (j + 1) * DH] = piece[:, columns].T
        side_t = jnp.where(line == j, lse[:, columns], side_t)
        side_t = jnp.where(line == GROUP + j, delta[:, columns], side_t)
    res_ref[:, SIDE:] = side_t.T


def far_kernel(q_ref, do_ref, key_ref, value_ref, both_ref, prob_ref, moved_ref, back_ref, side_ref):
    j = pl.program_id(0)
    q_t = q_ref[...].astype(F32).T.astype(BF)
    do_t = do_ref[...].astype(F32).T.astype(BF)
    prob, moved, out_t, grad_t, key_sum_t, lse, delta = attend(
        q_t, do_t, key_ref[...], value_ref[...], both_ref[...], None
    )
    prob_ref[...] = prob
    moved_ref[...] = moved
    for part, piece in enumerate((out_t, grad_t, key_sum_t)):
        at = pl.multiple_of(part * WIDTH + j * DH, DH)
        back_ref[:, pl.ds(at, DH)] = piece.T.astype(BF)
    line = lax.broadcasted_iota(jnp.int32, (DH, SLOTS), 0) - 8 * j
    side_t = jnp.zeros((DH, SLOTS), F32)
    for at, part in enumerate(split3(lse) + split3(delta)):
        side_t = jnp.where(line == at, part.astype(F32), side_t)

    @pl.when(j == 0)
    def _():
        side_ref[...] = side_t

    @pl.when(j > 0)
    def _():
        side_ref[...] += side_t

    @pl.when(j == GROUP - 1)
    def _():
        back_ref[:, SIDE:] = side_ref[...].T.astype(BF)


def combine_kernel(got_ref, first_ref, second_ref, own_ref, rows_ref, send_ref, stats_ref, scaled_ref):
    got = got_ref[...]
    picks = (first_ref[...], second_ref[...])
    far = [dot(pick, got) for pick in picks]
    there = [jnp.sum(pick.astype(F32), axis=1, keepdims=True) > 0.5 for pick in picks]
    lane = lax.broadcasted_iota(jnp.int32, (QB, 128), 1)
    tiled = [jnp.zeros((QB, 128), F32) for _ in picks]
    for j in range(GROUP):
        head = [slice(part * WIDTH + j * DH, part * WIDTH + (j + 1) * DH) for part in range(3)]
        side = own_ref[:, SIDE:]
        lses = [side[:, j : j + 1]]
        deltas = [side[:, GROUP + j : GROUP + j + 1]]
        for piece, here in zip(far, there):
            parts = piece[:, SIDE + 8 * j : SIDE + 8 * j + 6]
            lse = parts[:, 0:1] + parts[:, 1:2] + parts[:, 2:3]
            lses.append(jnp.where(here, lse, NEG_FILL))
            deltas.append(parts[:, 3:4] + parts[:, 4:5] + parts[:, 5:6])
        top = jnp.maximum(jnp.maximum(lses[0], lses[1]), lses[2])
        total = sum(jnp.exp(lse - top) for lse in lses)
        logsum = top + jnp.log(total)
        shares = [jnp.exp(lse - logsum) for lse in lses]
        pieces = [own_ref[...]] + far
        out = sum(share * piece[:, head[0]] for share, piece in zip(shares, pieces)).astype(BF)
        q = rows_ref[:, j * DH : (j + 1) * DH].astype(F32)
        do = rows_ref[:, WIDTH + j * DH : WIDTH + (j + 1) * DH].astype(F32)
        delta = jnp.sum(out.astype(F32) * do, axis=1, keepdims=True)
        moves = [share * (own - delta) for share, own in zip(shares, deltas)]
        grad = sum(
            share * piece[:, head[1]] + move * piece[:, head[2]]
            for share, move, piece in zip(shares, moves, pieces)
        )
        send_ref[:, j * DH : (j + 1) * DH] = out
        send_ref[:, WIDTH + j * DH : WIDTH + (j + 1) * DH] = grad.astype(BF)
        at = slice(j * QB, (j + 1) * QB)
        scaled_ref[at, :DH] = (shares[0] * do).astype(BF)
        scaled_ref[at, DH : 2 * DH] = (moves[0] * q).astype(BF)
        scaled_ref[at, 2 * DH :] = (shares[0] * q).astype(BF)
        for e in range(2):
            tiled[e] = jnp.where(lane % 8 == j, shares[e + 1], tiled[e])
            tiled[e] = jnp.where(lane % 8 == GROUP + j, moves[e + 1], tiled[e])
    spread = jnp.zeros((SLOTS, 128), F32)
    for pick, values in zip(picks, tiled):
        for part in split3(values):
            spread = spread + dot_first(pick, part)
    rank = lax.broadcasted_iota(jnp.int32, (SLOTS, 128), 0) % CAP
    keep = lax.broadcasted_iota(jnp.int32, (SLOTS, 128), 1) // 8 == rank
    stats_ref[...] = jnp.sum(jnp.where(keep, spread, 0.0).reshape(NB, CAP, 128), axis=1)


def grads_kernel(
    stats_ref, q_ref, do_ref, prob_ref, moved_ref, own_prob_ref, own_moved_ref, scaled_ref,
    grad_k_ref, grad_v_ref, share_ref, sum_ref,
):
    j = pl.program_id(0)
    lane = lax.broadcasted_iota(jnp.int32, (SLOTS, 128), 1)

    @pl.when(j == 0)
    def _():
        rank = lax.broadcasted_iota(jnp.int32, (SLOTS, 128), 0) % CAP
        wide = jnp.broadcast_to(stats_ref[...][:, None, :], (NB, CAP, 128)).reshape(SLOTS, 128)
        wide = jnp.where(lane // 8 == rank, wide, 0.0)
        for step in (8, 16, 32, 64):
            wide = wide + pltpu.roll(wide, step, 1)
        share_ref[...] = wide

    stats = share_ref[...]
    share = jnp.sum(jnp.where(lane == j, stats, 0.0), axis=1, keepdims=True)
    move = jnp.sum(jnp.where(lane == GROUP + j, stats, 0.0), axis=1, keepdims=True)
    q = q_ref[...].astype(F32)
    do = do_ref[...].astype(F32)
    pair = jnp.concatenate([(share * do).astype(BF), (move * q).astype(BF)], axis=1)
    scaled = scaled_ref[...]
    first = dot(prob_ref[...], pair) + dot(own_prob_ref[...], scaled[:, : 2 * DH])
    second = dot(moved_ref[...], (share * q).astype(BF)) + dot(own_moved_ref[...], scaled[:, 2 * DH :])
    both = jnp.concatenate([first[:, :DH], first[:, DH:] + second], axis=1)

    @pl.when(j == 0)
    def _():
        sum_ref[...] = both

    @pl.when(j > 0)
    def _():
        sum_ref[...] += both

    @pl.when(j == GROUP - 1)
    def _():
        grad_v_ref[...] = sum_ref[:, :DH].astype(BF)
        grad_k_ref[...] = (sum_ref[:, DH:] * SCALE).astype(BF)


def unpack_kernel(got_ref, out_ref, dq_ref):
    for head in range(KVH):
        columns = slice(head * WIDTH, (head + 1) * WIDTH)
        out_ref[:, columns] = got_ref[head, :, :WIDTH]
        dq_ref[:, columns] = got_ref[head, :, WIDTH:]


def exchange(array, axis):
    return lax.all_to_all(array, axis, split_axis=0, concat_axis=0, tiled=True)


def on_device(queries, keys, values, grad_out, gates, block_order):
    packed = call(pack_kernel, shape((KVH, QB // KVH, 2 * WIDTH), BF))(queries, grad_out)
    first, second = call(route_kernel, [shape((QB, SLOTS), BF)] * 2)(
        gates.reshape(QB, 3), block_order.reshape(1, NB)
    )
    rows = exchange(packed, "head").reshape(QB, 2 * WIDTH)
    sent = call(gather_kernel, shape((SLOTS, 2 * WIDTH), BF))(rows, first, second)
    got = exchange(sent.reshape(NB, CAP, 2 * WIDTH), "ctx").reshape(SLOTS, 2 * WIDTH)
    own_prob, own_moved, own_res, both_t = call(
        own_kernel,
        [
            shape((BS, WIDTH), BF),
            shape((BS, WIDTH), BF),
            shape((QB, BACK), F32),
            shape((2 * DH, BS), BF),
        ],
    )(rows, keys, values)
    whole = lambda *dims: pl.BlockSpec(dims, lambda j: (0,) * len(dims))
    query_spec = pl.BlockSpec((SLOTS, DH), lambda j: (0, j))
    grad_spec = pl.BlockSpec((SLOTS, DH), lambda j: (0, GROUP + j))
    tall = lambda columns: pl.BlockSpec((BS, columns), lambda j: (0, j))
    prob, moved, back = call(
        far_kernel,
        [shape((BS, GROUP * SLOTS), BF), shape((BS, GROUP * SLOTS), BF), shape((SLOTS, BACK), BF)],
        grid=(GROUP,),
        in_specs=[query_spec, grad_spec, whole(BS, DH), whole(BS, DH), whole(2 * DH, BS)],
        out_specs=[tall(SLOTS), tall(SLOTS), whole(SLOTS, BACK)],
        scratch_shapes=[pltpu.VMEM((DH, SLOTS), F32)],
    )(got, got, keys, values, both_t)
    returned = exchange(back.reshape(NB, CAP, BACK), "ctx").reshape(SLOTS, BACK)
    send, stats, scaled = call(
        combine_kernel,
        [shape((QB, 2 * WIDTH), BF), shape((NB, 128), F32), shape((GROUP * QB, 3 * DH), BF)],
    )(returned, first, second, own_res, rows)
    stats_got = exchange(stats.reshape(NB, 1, 128), "ctx").reshape(NB, 128)
    tokens = exchange(send.reshape(KVH, QB // KVH, 2 * WIDTH), "head")
    grad_keys, grad_values = call(
        grads_kernel,
        [shape((BS, DH), BF), shape((BS, DH), BF)],
        grid=(GROUP,),
        in_specs=[
            whole(NB, 128),
            query_spec,
            grad_spec,
            tall(SLOTS),
            tall(SLOTS),
            tall(QB),
            tall(QB),
            pl.BlockSpec((QB, 3 * DH), lambda j: (j, 0)),
        ],
        out_specs=[whole(BS, DH), whole(BS, DH)],
        scratch_shapes=[pltpu.VMEM((SLOTS, 128), F32), pltpu.VMEM((BS, 2 * DH), F32)],
    )(stats_got, got, got, prob, moved, own_prob, own_moved, scaled)
    attn_out, grad_queries = call(unpack_kernel, [shape((QB // KVH, HQ * DH), BF)] * 2)(tokens)
    return attn_out, grad_queries, grad_keys, grad_values


def solution(mesh):
    return jax.shard_map(
        on_device,
        mesh=mesh,
        in_specs=(
            P(("ctx", "head"), None),
            P("ctx", "head"),
            P("ctx", "head"),
            P(("ctx", "head"), None),
            P("ctx", "head", None),
            P(),
        ),
        out_specs=(
            P(("ctx", "head"), None),
            P(("ctx", "head"), None),
            P("ctx", "head"),
            P("ctx", "head"),
        ),
        check_vma=False,
    )
```

time: 212 us -> 153 us (0.72)
  local copies, waits for them, and re-layouts: 65.5 us -> 3.8 us
  blocking collectives: 0 us -> 61.2 us
  starting transfers between devices: 77.5 us -> 24 us
  Pallas kernels: 0 us -> 37.2 us
  matrix products: 28.4 us -> 0 us
  other arithmetic: 10.4 us -> 0 us
    all_to_all x0 -> x2, blocking collectives: none -> 61.2 us  [exchange(): return lax.all_to_all(array, axis, split_axis=0, concat_axis=0, tiled=True)]
    all_to_all x11 -> x3, starting transfers between devices: 77.5 us -> 24 us  [exchange(): return lax.all_to_all(array, axis, split_axis=0, concat_axis=0, tiled=True)]
    pallas_call x0 -> x8, Pallas kernels: none -> 37.2 us  [the longest x1 12 us: on_device(): call(far_kernel, [shape((BS, GROUP * SLOTS), BF), shape((BS, GROUP * SLOT...]
    dot_general x12 -> x0, matrix products: 28.4 us -> none  [the longest x2 6.71 us: block_grads(): jnp.einsum('zhsc,zhsr->chr', gate_matrix.astype(jnp.bfloat16), gradient_r...]
    gather x7 -> x0, local copies, waits for them, and re-layouts: 19.4 us -> none  [the longest x4 14.8 us: pack(): picked = padded[source_row.T, slot_heads]]
    all_to_all x8 -> x0, local copies, waits for them, and re-layouts: 9.01 us -> none  [the longest x1 1.61 us: on_device(): lax.all_to_all(queries, 'head', split_axis=1, concat_axis=0, tiled=True)]
    another operation x13 -> x0, local copies, waits for them, and re-layouts: 8.57 us -> none
    convert_element_type x9 -> x0, local copies, waits for them, and re-layouts: 7.03 us -> none  [the longest x1 1.75 us: on_device(): grad4.astype(jnp.float32) * attention.astype(jnp.float32)]
  transfers between devices with their start and end apart: 11 -> 3, of which waited for: 7 -> 2; matrix products, arithmetic and copies ran while one was open for 40% -> 1% of each run, Pallas kernels for 0% -> 10%
where the time goes in v1:
time: 153 us; the launch traced here: 152 us
  blocking collectives  61.2 us (40%)
  Pallas kernels  37.2 us (24%)
  waiting for transfers between devices  24.8 us (16%)
  starting transfers between devices  24 us (16%)
  local copies, waits for them, and re-layouts  3.8 us (2%)
    all_to_all x2, blocking collectives, exchange(): return lax.all_to_all(array, axis, split_axis=0, concat_axis=0, tiled=True)  61.2 us
    all_to_all x3, waiting for transfers between devices, exchange(): return lax.all_to_all(array, axis, split_axis=0, concat_axis=0, tiled=True)  24.8 us
    all_to_all x3, starting transfers between devices, exchange(): return lax.all_to_all(array, axis, split_axis=0, concat_axis=0, tiled=True)  24 us
    pallas_call x1, Pallas kernels, on_device(): call(far_kernel, [shape((BS, GROUP * SLOTS), BF), shape((BS, GROUP * SLOT...  12 us
    pallas_call x1, Pallas kernels, on_device(): call(grads_kernel, [shape((BS, DH), BF), shape((BS, DH), BF)], grid=(GROU...  8.43 us
    pallas_call x1, Pallas kernels, on_device(): call(combine_kernel, [shape((QB, 2 * WIDTH), BF), shape((NB, 128), F32),...  4.79 us
    pallas_call x1, Pallas kernels, on_device(): call(own_kernel, [shape((BS, WIDTH), BF), shape((BS, WIDTH), BF), shape((...  4.16 us
    unnamed x7, local copies, waits for them, and re-layouts  3.8 us
  transfers between devices with their start and end apart: 3, of which 2 were waited for; matrix products, arithmetic and copies ran while one was open for 1% of the time, Pallas kernels for 10%

profile of v1, /device:TPU:1, one launch (start us, length us, event | category | flops | bytes accessed | tf_op | source)
XLA Modules:
  0.0 151.7 jit_solution(18144376970597262650)
XLA Ops:
  0.6 1.7 %shard_map.93 = bf16[8,16,1024]{2,1,0:T(8,128)(2,1)} custom-call(bf16[16,4096]{1,0:T(8,128)(2,1)} %q_ref.1, bf16[16,4096]{1,0:T(8,128)(2,1)} %do_ref.1), custom_call_target="tpu_custom_call" | custom-call | tf_op jit(solution)/shard_map/pallas_call | solution.py:268
  2.3 6.6 %all-to-all-start = ((bf16[8,16,1024]{2,1,0:T(8,128)(2,1)}), bf16[8,16,1024]{2,1,0:T(8,128)(2,1)S(1)}, u32[]{:S(2)}, u32[]{:S(2)}) async-start(bf16[8,16,1024]{2,1,0:T(8,128)(2,1)} %shard_map.93), calls=%async_computation | async-start | bytes 524288 | tf_op jit(solution)/shard_map/all_to_all | solution.py:264
  8.9 1.4 copy.11
  10.3 2.0 %shard_map.94 = (bf16[128,512]{1,0:T(8,128)(2,1)}, bf16[128,512]{1,0:T(8,128)(2,1)}) custom-call(s32[128,3]{1,0:T(8,128)} %bitcast.23, s32[1,32]{1,0:T(1,128)} %bitcast.26), custom_call_target="tpu_custom_call" | custom-call | tf_op jit(solution)/shard_map/pallas_call | solution.py:269
  12.3 3.1 %all-to-all-done = bf16[8,16,1024]{2,1,0:T(8,128)(2,1)S(1)} async-done(((bf16[8,16,1024]{2,1,0:T(8,128)(2,1)}), bf16[8,16,1024]{2,1,0:T(8,128)(2,1)S(1)}, u32[]{:S(2)}, u32[]{:S(2)}) %all-to-all-start) | async-done | bytes 262176 | tf_op jit(solution)/shard_map/all_to_all | solution.py:264
  15.4 0.0 copy-start.1
  15.4 0.7 copy-done.1
  16.1 2.5 %shard_map.95 = bf16[512,1024]{1,0:T(8,128)(2,1)} custom-call(bf16[128,1024]{1,0:T(8,128)(2,1)} %bitcast.17, bf16[128,512]{1,0:T(8,128)(2,1)} %get-tuple-element.20.first_ref, bf16[128,512]{1,0:T(8,128)(2,1)} %get-tuple-element.21.second_ref), custom_call_target="tpu_custom_call" | custom-call | tf_op jit(solution)/shard_map/pallas_call | solution.py:273
  18.6 10.4 %all-to-all-start.1 = ((bf16[32,16,1024]{2,1,0:T(8,128)(2,1)}), bf16[32,16,1024]{2,1,0:T(8,128)(2,1)S(1)}, u32[]{:S(2)}, u32[]{:S(2)}) async-start(bf16[32,16,1024]{2,1,0:T(8,128)(2,1)} %bitcast.20), calls=%async_computation.1 | async-start | bytes 2097152 | tf_op jit(solution)/shard_map/all_to_all | solution.py:264
  29.0 4.2 %shard_map.96 = (bf16[1024,512]{1,0:T(8,128)(2,1)}, bf16[1024,512]{1,0:T(8,128)(2,1)}, f32[128,1664]{1,0:T(8,128)}, bf16[256,1024]{1,0:T(8,128)(2,1)}) custom-call(bf16[128,1024]{1,0:T(8,128)(2,1)} %bitcast.18, bf16[1024,128]{1,0:T(8,128)(2,1)} %key_ref.3, bf16[1024,128]{1,0:T(8,128)(2,1)} %value_ref.3), custom_call_target="tpu_custom_call" | custom-call | tf_op jit(solution)/shard_map/pallas_call | solution.py:275
  33.2 21.7 %all-to-all-done.1 = bf16[32,16,1024]{2,1,0:T(8,128)(2,1)S(1)} async-done(((bf16[32,16,1024]{2,1,0:T(8,128)(2,1)}), bf16[32,16,1024]{2,1,0:T(8,128)(2,1)S(1)}, u32[]{:S(2)}, u32[]{:S(2)}) %all-to-all-start.1) | async-done | bytes 1048608 | tf_op jit(solution)/shard_map/all_to_all | solution.py:264
  54.9 0.0 copy-start
  54.9 1.0 copy-done
  55.8 12.0 %shard_map.97 = (bf16[1024,2048]{1,0:T(8,128)(2,1)}, bf16[1024,2048]{1,0:T(8,128)(2,1)}, bf16[512,1664]{1,0:T(8,128)(2,1)}) custom-call(bf16[512,1024]{1,0:T(8,128)(2,1)} %bitcast.12, bf16[512,1024]{1,0:T(8,128)(2,1)} %bitcast.13, bf16[1024,128]{1,0:T(8,128)(2,1)} %key_ref.3, bf16[1024,128]{1,0:T(8,128)(2,1)} %value_ref.3, ...), custom_call_target="tpu_custom_call" | custom-call | tf_op jit(solution)/shard_map/pallas_call | solution.py:288
  67.8 46.2 %all_to_all.25 = bf16[32,16,1664]{2,1,0:T(8,128)(2,1)} all-to-all(bf16[32,16,1664]{2,1,0:T(8,128)(2,1)} %bitcast.21), channel_id=1, replica_groups=mesh['ctx'=32,'head'=8] {'ctx'}, dimensions={0} | all-to-all | bytes 3407872 | tf_op jit(solution)/shard_map/all_to_all | solution.py:264
  114.0 4.8 %shard_map.98 = (bf16[128,1024]{1,0:T(8,128)(2,1)}, f32[32,128]{1,0:T(8,128)}, bf16[512,384]{1,0:T(8,128)(2,1)}) custom-call(bf16[512,1664]{1,0:T(8,128)(2,1)} %bitcast.16, bf16[128,512]{1,0:T(8,128)(2,1)} %get-tuple-element.20.first_ref, bf16[128,512]{1,0:T(8,128)(2,1)} %get-tuple-element.21.second_ref, f32[128,1664]{1,0:T(8,128)} %get-tuple-element.24.own_ref, ...), custom_call_target="tpu_custom_call" | custom-call | tf_op jit(solution)/shard_map/pallas_call | solution.py:297
  118.8 15.1 %all_to_all.26 = f32[32,1,128]{2,1,0:T(1,128)} all-to-all(f32[32,1,128]{2,1,0:T(1,128)} %bitcast.25), channel_id=1, replica_groups=mesh['ctx'=32,'head'=8] {'ctx'}, dimensions={0} | all-to-all | bytes 32768 | tf_op jit(solution)/shard_map/all_to_all | solution.py:264
  133.8 7.1 %all-to-all-start.3 = ((bf16[8,16,1024]{2,1,0:T(8,128)(2,1)}), bf16[8,16,1024]{2,1,0:T(8,128)(2,1)S(1)}, u32[]{:S(2)}, u32[]{:S(2)}) async-start(bf16[8,16,1024]{2,1,0:T(8,128)(2,1)} %bitcast.22), calls=%async_computation.3 | async-start | bytes 524288 | tf_op jit(solution)/shard_map/all_to_all | solution.py:264
  140.9 8.4 %shard_map.100 = (bf16[1024,128]{1,0:T(8,128)(2,1)}, bf16[1024,128]{1,0:T(8,128)(2,1)}) custom-call(f32[32,128]{1,0:T(8,128)} %bitcast.24, bf16[512,1024]{1,0:T(8,128)(2,1)} %bitcast.14, bf16[512,1024]{1,0:T(8,128)(2,1)} %bitcast.15, bf16[1024,2048]{1,0:T(8,128)(2,1)} %get-tuple-element.29.prob_ref, bf16[1024,2048]{1,0:T(8,128)(2,1)} %get-tuple-element.30.moved_ref, ...), custom_call_target="tpu_custom_call" | custom-call | tf_op jit(solution)/shard_map/pallas_call | solution.py:303
  149.3 0.0 all-to-all-done.3.got_ref
  149.3 0.0 copy-start.2
  149.4 0.7 copy-done.2
  150.0 1.7 %shard_map.99 = (bf16[16,4096]{1,0:T(8,128)(2,1)}, bf16[16,4096]{1,0:T(8,128)(2,1)}) custom-call(bf16[8,16,1024]{2,1,0:T(8,128)(2,1)} %copy-done.2), custom_call_target="tpu_custom_call" | custom-call | tf_op jit(solution)/shard_map/pallas_call | solution.py:320
Async XLA Ops:
  2.3 13.1 %all-to-all-start = ((bf16[8,16,1024]{2,1,0:T(8,128)(2,1)}), bf16[8,16,1024]{2,1,0:T(8,128)(2,1)S(1)}, u32[]{:S(2)}, u32[]{:S(2)}) async-start(bf16[8,16,1024]{2,1,0:T(8,128)(2,1)} %shard_map.93), calls=%async_computation | async-start | bytes 524288 | tf_op jit(solution)/shard_map/all_to_all | solution.py:264
  15.4 0.7 copy-start.1
  18.6 36.3 %all-to-all-start.1 = ((bf16[32,16,1024]{2,1,0:T(8,128)(2,1)}), bf16[32,16,1024]{2,1,0:T(8,128)(2,1)S(1)}, u32[]{:S(2)}, u32[]{:S(2)}) async-start(bf16[32,16,1024]{2,1,0:T(8,128)(2,1)} %bitcast.20), calls=%async_computation.1 | async-start | bytes 2097152 | tf_op jit(solution)/shard_map/all_to_all | solution.py:264
  54.9 1.0 copy-start
  133.8 15.5 %all-to-all-start.3 = ((bf16[8,16,1024]{2,1,0:T(8,128)(2,1)}), bf16[8,16,1024]{2,1,0:T(8,128)(2,1)S(1)}, u32[]{:S(2)}, u32[]{:S(2)}) async-start(bf16[8,16,1024]{2,1,0:T(8,128)(2,1)} %bitcast.22), calls=%async_computation.3 | async-start | bytes 524288 | tf_op jit(solution)/shard_map/all_to_all | solution.py:264
  149.3 0.7 copy-start.2
